TPU v7x, 128 devices: a whole 4x4x4 slice. The times are simulated.
128 devices in a mesh: gx: 8 (over y, core), gy: 16 (over z, x).
Axes of the slice: x: 4, y: 4, z: 4, core: 2. Of those that a mesh axis runs over, the one named last changes fastest.
Arguments:
- level_set: float32 [512, 64, 4096], P(('gx', 'gy')), may hold values from -8 to 8
- tile_count: int32 [128], P(('gx', 'gy')), may hold values from 2 to 4, as said below
- neighbours: int32 [512, 6], P(('gx', 'gy')), may hold values from -1 to 7, as said below
Outputs:
- redistanced: float32 [512, 64, 4096], P(('gx', 'gy'))
Inputs may be any that keep to these rules, and one draw needn't show every extreme that they name: Band tiles of a device fill its slots 0 to tile_count - 1; the other slots are empty. Some device holds 4. `neighbours`: -1 means no band tile on that face. A value n below 4 is slot n of the same device; a value n of 4 or more is slot n - 4 of the device one step lower along gx (face 0), higher along gx (face 1), lower along gy (face 2) or higher along gy (face 3), which exists; faces 4 and 5 (third dimension) are -1 or below 4. Every listed slot holds a band tile and is never the tile itself; empty slots list -1.
All inputs are finite; a program needn't handle non-finite values.
Results may differ from a plain program's by a relative error of at most 0.0003.
Values sent between devices are 32-bit elements; how exact they have to be, the bound alone decides.
A program may use at most 192 MiB of HBM per device.

v0:
```python
import jax
import jax.numpy as jnp
from jax import lax
from jax.sharding import PartitionSpec as P

weno_eps = 1e-06
pseudo_step = 0.3


def padded_2(block, sides, width):
    for axis, dim in sides:
        count = lax.axis_size(axis)
        forward = [(i, i + 1) for i in range(count - 1)]
        backward = [(target, source) for source, target in forward]
        low = lax.ppermute(
            lax.slice_in_dim(block, block.shape[dim] - width, None, axis=dim), axis, forward
        )
        high = lax.ppermute(lax.slice_in_dim(block, 0, width, axis=dim), axis, backward)
        block = jnp.concatenate([low, block, high], axis=dim)
    return block


def smooth_part(diff_a, diff_b, diff_c, diff_d, diff_e):
    stencil_one = diff_a / 3.0 - 7.0 * diff_b / 6.0 + 11.0 * diff_c / 6.0
    stencil_two = -diff_b / 6.0 + 5.0 * diff_c / 6.0 + diff_d / 3.0
    stencil_three = diff_c / 3.0 + 5.0 * diff_d / 6.0 - diff_e / 6.0
    beta_one = 13.0 / 12.0 * jnp.square(diff_a - 2.0 * diff_b + diff_c) + 0.25 * jnp.square(
        diff_a - 4.0 * diff_b + 3.0 * diff_c
    )
    beta_two = 13.0 / 12.0 * jnp.square(diff_b - 2.0 * diff_c + diff_d) + 0.25 * jnp.square(
        diff_b - diff_d
    )
    beta_three = 13.0 / 12.0 * jnp.square(diff_c - 2.0 * diff_d + diff_e) + 0.25 * jnp.square(
        3.0 * diff_c - 4.0 * diff_d + diff_e
    )
    alpha_one = 0.1 / jnp.square(weno_eps + beta_one)
    alpha_two = 0.6 / jnp.square(weno_eps + beta_two)
    alpha_three = 0.3 / jnp.square(weno_eps + beta_three)
    return (alpha_one * stencil_one + alpha_two * stencil_two + alpha_three * stencil_three) / (
        alpha_one + alpha_two + alpha_three
    )


def all_layers(tile_flat):
    edge_size = tile_flat.shape[0]
    cube_view = tile_flat.reshape(edge_size, edge_size, edge_size)
    stacked = [tile_flat[:3], tile_flat[edge_size - 3 :]]
    for low_part in [cube_view[:, :3, :], cube_view[:, edge_size - 3 :, :]]:
        stacked.append(jnp.transpose(low_part, (1, 0, 2)).reshape(3, edge_size * edge_size))
    for low_part in [cube_view[:, :, :3], cube_view[:, :, edge_size - 3 :]]:
        stacked.append(jnp.transpose(low_part, (2, 0, 1)).reshape(3, edge_size * edge_size))
    return jnp.stack(stacked)


def one_sided(padded, axis):
    width = padded.shape[axis]
    diffs = lax.slice_in_dim(padded, 1, width, axis=axis) - lax.slice_in_dim(
        padded, 0, width - 1, axis=axis
    )
    inner = width - 6
    parts = [lax.slice_in_dim(diffs, k, k + inner, axis=axis) for k in range(6)]
    minus_side = smooth_part(parts[0], parts[1], parts[2], parts[3], parts[4])
    plus_side = smooth_part(parts[5], parts[4], parts[3], parts[2], parts[1])
    return (minus_side, plus_side)


def upwind_square(minus_side, plus_side, sign_part):
    outward = jnp.maximum(
        jnp.square(jnp.maximum(minus_side, 0.0)), jnp.square(jnp.minimum(plus_side, 0.0))
    )
    inward = jnp.maximum(
        jnp.square(jnp.minimum(minus_side, 0.0)), jnp.square(jnp.maximum(plus_side, 0.0))
    )
    return jnp.where(sign_part > 0.0, outward, inward)


def tile_rate(tile_flat, halo_layers, sign_tile):
    edge_size = tile_flat.shape[0]
    padded = jnp.concatenate([halo_layers[0], tile_flat, halo_layers[1]], axis=0)
    minus_side, plus_side = one_sided(padded, 0)
    squares = upwind_square(minus_side, plus_side, sign_tile).reshape(
        edge_size, edge_size, edge_size
    )
    cube_view = tile_flat.reshape(edge_size, edge_size, edge_size)
    sign_cube = sign_tile.reshape(edge_size, edge_size, edge_size)
    low_y = jnp.transpose(halo_layers[2].reshape(3, edge_size, edge_size), (1, 0, 2))
    high_y = jnp.transpose(halo_layers[3].reshape(3, edge_size, edge_size), (1, 0, 2))
    padded = jnp.concatenate([low_y, cube_view, high_y], axis=1)
    minus_side, plus_side = one_sided(padded, 1)
    squares = squares + upwind_square(minus_side, plus_side, sign_cube)
    low_z = jnp.transpose(halo_layers[4].reshape(3, edge_size, edge_size), (1, 2, 0))
    high_z = jnp.transpose(halo_layers[5].reshape(3, edge_size, edge_size), (1, 2, 0))
    padded = jnp.concatenate([low_z, cube_view, high_z], axis=2)
    minus_side, plus_side = one_sided(padded, 2)
    squares = squares + upwind_square(minus_side, plus_side, sign_cube)
    return -sign_tile * (jnp.sqrt(squares.reshape(edge_size, edge_size * edge_size)) - 1.0)


def gathered_halos(level_field, neighbours):
    layer_stack = jax.vmap(all_layers)(level_field)
    x_pair = jnp.stack([layer_stack[:, 0], layer_stack[:, 1]])
    x_wide = padded_2(x_pair, (("gx", 0),), 1)
    y_pair = jnp.stack([layer_stack[:, 2], layer_stack[:, 3]])
    y_wide = padded_2(y_pair, (("gy", 0),), 1)
    tables = [
        jnp.concatenate([layer_stack[:, 1], x_wide[0]], axis=0),
        jnp.concatenate([layer_stack[:, 0], x_wide[3]], axis=0),
        jnp.concatenate([layer_stack[:, 3], y_wide[0]], axis=0),
        jnp.concatenate([layer_stack[:, 2], y_wide[3]], axis=0),
        layer_stack[:, 5],
        layer_stack[:, 4],
    ]
    halo_list = []
    for face_index in range(6):
        face_codes = neighbours[:, face_index]
        table_rows = tables[face_index].shape[0]
        picked = jnp.take(tables[face_index], jnp.clip(face_codes, 0, table_rows - 1), axis=0)
        upper_side = face_index % 2
        edge_rows = (
            layer_stack[:, face_index, 2] if upper_side == 1 else layer_stack[:, face_index, 0]
        )
        border = jnp.broadcast_to(edge_rows[:, None, :], picked.shape)
        halo_list.append(jnp.where((face_codes < 0)[:, None, None], border, picked))
    return jnp.stack(halo_list, axis=1)


def rate_range(level_field, halo_all, sign_field, begin, finish):

    def one_tile(tile_index, totals):
        tile_flat = lax.dynamic_index_in_dim(level_field, tile_index, 0, keepdims=False)
        halo_layers = lax.dynamic_index_in_dim(halo_all, tile_index, 0, keepdims=False)
        sign_tile = lax.dynamic_index_in_dim(sign_field, tile_index, 0, keepdims=False)
        return lax.dynamic_update_index_in_dim(
            totals, tile_rate(tile_flat, halo_layers, sign_tile), tile_index, 0
        )

    return lax.fori_loop(begin, finish, one_tile, jnp.zeros_like(level_field))


def local(level_set, tile_count, neighbours):
    slots = level_set.shape[0]
    live_count = tile_count[0]
    sign_field = level_set / jnp.sqrt(jnp.square(level_set) + 1.0)
    positions = jnp.arange(slots, dtype=jnp.int32)

    def rates(level_field):
        halo_all = gathered_halos(level_field, neighbours)
        return rate_range(level_field, halo_all, sign_field, 0, live_count)

    section_one = level_set + pseudo_step * rates(level_set)
    section_two = 0.75 * level_set + 0.25 * (section_one + pseudo_step * rates(section_one))
    section_three = level_set / 3.0 + 2.0 / 3.0 * (section_two + pseudo_step * rates(section_two))
    live_mask = positions < live_count
    return jnp.where(live_mask[:, None, None], section_three, 0.0)


def solution(mesh):
    placed = (P(("gx", "gy"), None, None), P(("gx", "gy")), P(("gx", "gy"), None))
    return jax.shard_map(
        local, mesh=mesh, in_specs=placed, out_specs=P(("gx", "gy"), None, None), check_vma=False
    )
```

profile of v0, /device:TPU:2, one launch (start us, length us, event | category | flops | bytes accessed | tf_op | source)
XLA Modules:
  0.0 927.7 jit_solution(3207695523577234691)
XLA Ops:
  0.0 7.9 reshape.311
  10.7 13.2 %fusion.11 = (f32[4,64,64,3]{3,2,1,0:T(8,128)}, f32[4,64,64,3]{3,2,1,0:T(8,128)}) fusion(f32[4,64,64,64]{3,2,1,0:T(8,128)} %reshape.311), kind=kLoop, calls=%fused_computation.226 | loop fusion | bytes 786432 | tf_op jit(solution)/shard_map/vmap()/slice | solution.py:50
  82.4 225.7 %while.39 = (s32[]{:T(128)}, f32[4,64,4096]{2,1,0:T(8,128)}, s32[]{:T(128)}, f32[4,64,4096]{2,1,0:T(8,128)}, f32[4,6,3,4096]{3,2,0,1:T(4,128)}, /*index=5*/f32[4...) while((s32[]{:T(128)}, f32[4,64,4096]{2,1,0:T(8,128)}, s32[]{:T(128)}, f32[4,64,4096]{2,1,0:T(8,128)}, ...), condition=%wide.region_1.4_spmd, body=%wide.region_0.0_spmd.sunk | while | flops 110309376 | bytes 66207976 | solution.py:137
  112.1 22.2 %sqrt_add_fusion.6 = f32[64,64,64]{2,1,0:T(8,128)} fusion(pred[64,64,64]{2,1,0:T(8,128)(4,1)S(1)} %copy-done.7, f32[64,64,69]{2,1,0:T(8,128)S(1)} %slice_subtract_fusion.19, f32[64,64,64]{2,1,0:T(8,128)S(1)} %copy-done.4, f32[64,69,64]{2,1,0:T(8,128)S(1)} %slice_subtract_fusion.20), kind=kLoop, calls=%fused_computation.22.clone.1 | loop fusion | flops 71565312 | bytes 14942208 | tf_op jit(solution)/shard_map/while/body/sub | solution.py:96
  168.2 22.2 %sqrt_add_fusion.6 = f32[64,64,64]{2,1,0:T(8,128)} fusion(pred[64,64,64]{2,1,0:T(8,128)(4,1)S(1)} %copy-done.7, f32[64,64,69]{2,1,0:T(8,128)S(1)} %slice_subtract_fusion.19, f32[64,64,64]{2,1,0:T(8,128)S(1)} %copy-done.4, f32[64,69,64]{2,1,0:T(8,128)S(1)} %slice_subtract_fusion.20), kind=kLoop, calls=%fused_computation.22.clone.1 | loop fusion | flops 71565312 | bytes 14942208 | tf_op jit(solution)/shard_map/while/body/sub | solution.py:96
  198.2 6.3 maximum_select_fusion.6
  224.3 22.2 %sqrt_add_fusion.6 = f32[64,64,64]{2,1,0:T(8,128)} fusion(pred[64,64,64]{2,1,0:T(8,128)(4,1)S(1)} %copy-done.7, f32[64,64,69]{2,1,0:T(8,128)S(1)} %slice_subtract_fusion.19, f32[64,64,64]{2,1,0:T(8,128)S(1)} %copy-done.4, f32[64,69,64]{2,1,0:T(8,128)S(1)} %slice_subtract_fusion.20), kind=kLoop, calls=%fused_computation.22.clone.1 | loop fusion | flops 71565312 | bytes 14942208 | tf_op jit(solution)/shard_map/while/body/sub | solution.py:96
  280.4 22.2 %sqrt_add_fusion.6 = f32[64,64,64]{2,1,0:T(8,128)} fusion(pred[64,64,64]{2,1,0:T(8,128)(4,1)S(1)} %copy-done.7, f32[64,64,69]{2,1,0:T(8,128)S(1)} %slice_subtract_fusion.19, f32[64,64,64]{2,1,0:T(8,128)S(1)} %copy-done.4, f32[64,69,64]{2,1,0:T(8,128)S(1)} %slice_subtract_fusion.20), kind=kLoop, calls=%fused_computation.22.clone.1 | loop fusion | flops 71565312 | bytes 14942208 | tf_op jit(solution)/shard_map/while/body/sub | solution.py:96
  314.3 7.9 reshape.316
  322.2 13.2 %fusion.9 = (f32[4,64,64,3]{3,2,1,0:T(8,128)}, f32[4,64,64,3]{3,2,1,0:T(8,128)}) fusion(f32[4,64,64,64]{3,2,1,0:T(8,128)} %reshape.316), kind=kLoop, calls=%fused_computation.224 | loop fusion | bytes 786432 | tf_op jit(solution)/shard_map/vmap()/slice | solution.py:50
  386.7 226.2 %while.40 = (s32[]{:T(128)}, f32[4,64,4096]{2,1,0:T(8,128)}, s32[]{:T(128)}, f32[4,64,4096]{2,1,0:T(8,128)}, f32[4,6,3,4096]{3,2,0,1:T(4,128)}, /*index=5*/f32[4...) while((s32[]{:T(128)}, f32[4,64,4096]{2,1,0:T(8,128)}, s32[]{:T(128)}, f32[4,64,4096]{2,1,0:T(8,128)}, ...), condition=%wide.region_3.6_spmd, body=%wide.region_2.5_spmd.sunk | while | flops 110309376 | bytes 66207976 | solution.py:137
  416.5 22.2 %sqrt_add_fusion.7 = f32[64,64,64]{2,1,0:T(8,128)} fusion(pred[64,64,64]{2,1,0:T(8,128)(4,1)S(1)} %copy-done.8, f32[64,64,69]{2,1,0:T(8,128)S(1)} %slice_subtract_fusion.22, f32[64,64,64]{2,1,0:T(8,128)S(1)} %copy-done.5, f32[64,69,64]{2,1,0:T(8,128)S(1)} %slice_subtract_fusion.23), kind=kLoop, calls=%fused_computation.36.clone.1 | loop fusion | flops 71565312 | bytes 14942208 | tf_op jit(solution)/shard_map/while/body/sub | solution.py:96
  472.8 22.2 %sqrt_add_fusion.7 = f32[64,64,64]{2,1,0:T(8,128)} fusion(pred[64,64,64]{2,1,0:T(8,128)(4,1)S(1)} %copy-done.8, f32[64,64,69]{2,1,0:T(8,128)S(1)} %slice_subtract_fusion.22, f32[64,64,64]{2,1,0:T(8,128)S(1)} %copy-done.5, f32[64,69,64]{2,1,0:T(8,128)S(1)} %slice_subtract_fusion.23), kind=kLoop, calls=%fused_computation.36.clone.1 | loop fusion | flops 71565312 | bytes 14942208 | tf_op jit(solution)/shard_map/while/body/sub | solution.py:96
  529.1 22.2 %sqrt_add_fusion.7 = f32[64,64,64]{2,1,0:T(8,128)} fusion(pred[64,64,64]{2,1,0:T(8,128)(4,1)S(1)} %copy-done.8, f32[64,64,69]{2,1,0:T(8,128)S(1)} %slice_subtract_fusion.22, f32[64,64,64]{2,1,0:T(8,128)S(1)} %copy-done.5, f32[64,69,64]{2,1,0:T(8,128)S(1)} %slice_subtract_fusion.23), kind=kLoop, calls=%fused_computation.36.clone.1 | loop fusion | flops 71565312 | bytes 14942208 | tf_op jit(solution)/shard_map/while/body/sub | solution.py:96
  585.4 22.2 %sqrt_add_fusion.7 = f32[64,64,64]{2,1,0:T(8,128)} fusion(pred[64,64,64]{2,1,0:T(8,128)(4,1)S(1)} %copy-done.8, f32[64,64,69]{2,1,0:T(8,128)S(1)} %slice_subtract_fusion.22, f32[64,64,64]{2,1,0:T(8,128)S(1)} %copy-done.5, f32[64,69,64]{2,1,0:T(8,128)S(1)} %slice_subtract_fusion.23), kind=kLoop, calls=%fused_computation.36.clone.1 | loop fusion | flops 71565312 | bytes 14942208 | tf_op jit(solution)/shard_map/while/body/sub | solution.py:96
  612.9 8.3 multiply_add_fusion
  621.2 7.9 reshape.321
  629.1 13.2 %fusion.7 = (f32[4,64,64,3]{3,2,1,0:T(8,128)}, f32[4,64,64,3]{3,2,1,0:T(8,128)}) fusion(f32[4,64,64,64]{3,2,1,0:T(8,128)} %reshape.321), kind=kLoop, calls=%fused_computation.222 | loop fusion | bytes 786432 | tf_op jit(solution)/shard_map/vmap()/slice | solution.py:50
  692.8 226.0 %while.41 = (s32[]{:T(128)}, f32[4,64,4096]{2,1,0:T(8,128)}, s32[]{:T(128)}, f32[4,64,4096]{2,1,0:T(8,128)}, f32[4,6,3,4096]{3,2,0,1:T(4,128)}, /*index=5*/f32[4...) while((s32[]{:T(128)}, f32[4,64,4096]{2,1,0:T(8,128)}, s32[]{:T(128)}, f32[4,64,4096]{2,1,0:T(8,128)}, ...), condition=%wide.region_5.8_spmd, body=%wide.region_4.7_spmd.sunk | while | flops 110309376 | bytes 66207976 | solution.py:137
  722.7 22.2 %sqrt_add_fusion.8 = f32[64,64,64]{2,1,0:T(8,128)} fusion(pred[64,64,64]{2,1,0:T(8,128)(4,1)S(1)} %copy-done.9, f32[64,64,69]{2,1,0:T(8,128)S(1)} %slice_subtract_fusion.25, f32[64,64,64]{2,1,0:T(8,128)S(1)} %copy-done.6, f32[64,69,64]{2,1,0:T(8,128)S(1)} %slice_subtract_fusion.26), kind=kLoop, calls=%fused_computation.50.clone.1 | loop fusion | flops 71565312 | bytes 14942208 | tf_op jit(solution)/shard_map/while/body/sub | solution.py:96
  779.0 22.2 %sqrt_add_fusion.8 = f32[64,64,64]{2,1,0:T(8,128)} fusion(pred[64,64,64]{2,1,0:T(8,128)(4,1)S(1)} %copy-done.9, f32[64,64,69]{2,1,0:T(8,128)S(1)} %slice_subtract_fusion.25, f32[64,64,64]{2,1,0:T(8,128)S(1)} %copy-done.6, f32[64,69,64]{2,1,0:T(8,128)S(1)} %slice_subtract_fusion.26), kind=kLoop, calls=%fused_computation.50.clone.1 | loop fusion | flops 71565312 | bytes 14942208 | tf_op jit(solution)/shard_map/while/body/sub | solution.py:96
  835.3 22.2 %sqrt_add_fusion.8 = f32[64,64,64]{2,1,0:T(8,128)} fusion(pred[64,64,64]{2,1,0:T(8,128)(4,1)S(1)} %copy-done.9, f32[64,64,69]{2,1,0:T(8,128)S(1)} %slice_subtract_fusion.25, f32[64,64,64]{2,1,0:T(8,128)S(1)} %copy-done.6, f32[64,69,64]{2,1,0:T(8,128)S(1)} %slice_subtract_fusion.26), kind=kLoop, calls=%fused_computation.50.clone.1 | loop fusion | flops 71565312 | bytes 14942208 | tf_op jit(solution)/shard_map/while/body/sub | solution.py:96
  891.6 22.2 %sqrt_add_fusion.8 = f32[64,64,64]{2,1,0:T(8,128)} fusion(pred[64,64,64]{2,1,0:T(8,128)(4,1)S(1)} %copy-done.9, f32[64,64,69]{2,1,0:T(8,128)S(1)} %slice_subtract_fusion.25, f32[64,64,64]{2,1,0:T(8,128)S(1)} %copy-done.6, f32[64,69,64]{2,1,0:T(8,128)S(1)} %slice_subtract_fusion.26), kind=kLoop, calls=%fused_computation.50.clone.1 | loop fusion | flops 71565312 | bytes 14942208 | tf_op jit(solution)/shard_map/while/body/sub | solution.py:96
  918.9 8.4 add_select_fusion
  (627 shorter events, 560.3 us)
Async XLA Ops:
  37.4 13.0 %copy-start.10 = (s32[4,6]{1,0:T(4,128)S(1)}, s32[4,6]{1,0:T(4,128)}, u32[]{:S(2)}) copy-start(s32[4,6]{1,0:T(4,128)} %param.15) | copy-start | bytes 292
  37.4 16.4 %copy-start.3 = (f32[4,64,4096]{2,1,0:T(8,128)S(1)}, f32[4,64,4096]{2,1,0:T(8,128)}, u32[]{:S(2)}) copy-start(f32[4,64,4096]{2,1,0:T(8,128)} %param.13) | copy-start | bytes 12582916
  39.0 25.8 %collective-permute-start = (f32[1,4,3,4096]{3,2,1,0:T(4,128)}, f32[1,4,3,4096]{3,2,1,0:T(4,128)}, u32[]{:S(2)}, u32[]{:S(2)}) collective-permute-start(f32[1,4,3,4096]{3,2,1,0:T(4,128)} %get-tuple-element.565), channel_id=1, source_target_pairs={{0,16},{16,32},{32,48},{48,64},{64,80},{80,96},{96,112},{1,17},{17... | collective-permute-start | bytes 589832 | tf_op jit(solution)/shard_map/ppermute | solution.py:15
  41.5 24.3 %collective-permute-start.1 = (f32[1,4,3,4096]{3,2,1,0:T(4,128)}, f32[1,4,3,4096]{3,2,1,0:T(4,128)}, u32[]{:S(2)}, u32[]{:S(2)}) collective-permute-start(f32[1,4,3,4096]{3,2,1,0:T(4,128)} %get-tuple-element.566), channel_id=1, source_target_pairs={{16,0},{32,16},{48,32},{64,48},{80,64},{96,80},{112,96},{17,1},{33... | collective-permute-start | bytes 589832 | tf_op jit(solution)/shard_map/ppermute | solution.py:18
  42.8 24.1 %collective-permute-start.2 = (f32[1,4,3,4096]{3,2,1,0:T(4,128)}, f32[1,4,3,4096]{3,2,1,0:T(4,128)}, u32[]{:S(2)}, u32[]{:S(2)}) collective-permute-start(f32[1,4,3,4096]{3,2,1,0:T(4,128)} %get-tuple-element.567), channel_id=1, source_target_pairs={{0,1},{1,2},{2,3},{3,4},{4,5},{5,6},{6,7},{7,8},{8,9},{9,10},{10,1... | collective-permute-start | bytes 589832 | tf_op jit(solution)/shard_map/ppermute | solution.py:15
  46.2 24.6 %collective-permute-start.3 = (f32[1,4,3,4096]{3,2,1,0:T(4,128)}, f32[1,4,3,4096]{3,2,1,0:T(4,128)}, u32[]{:S(2)}, u32[]{:S(2)}) collective-permute-start(f32[1,4,3,4096]{3,2,1,0:T(4,128)} %get-tuple-element.568), channel_id=1, source_target_pairs={{1,0},{2,1},{3,2},{4,3},{5,4},{6,5},{7,6},{8,7},{9,8},{10,9},{11,1... | collective-permute-start | bytes 589832 | tf_op jit(solution)/shard_map/ppermute | solution.py:18
  52.1 23.7 %copy-start.36 = (pred[4]{0:T(512)(128)(4,1)}, pred[4]{0:T(512)(128)(4,1)S(1)}, u32[]{:S(2)}) copy-start(pred[4]{0:T(512)(128)(4,1)S(1)} %get-tuple-element.444) | copy-start | bytes 16
  52.1 25.1 %copy-start.33 = (pred[4]{0:T(512)(128)(4,1)}, pred[4]{0:T(512)(128)(4,1)S(1)}, u32[]{:S(2)}) copy-start(pred[4]{0:T(512)(128)(4,1)S(1)} %get-tuple-element.443) | copy-start | bytes 16
  52.1 26.0 %copy-start.30 = (pred[4]{0:T(512)(128)(4,1)}, pred[4]{0:T(512)(128)(4,1)S(1)}, u32[]{:S(2)}) copy-start(pred[4]{0:T(512)(128)(4,1)S(1)} %get-tuple-element.447) | copy-start | bytes 16
  52.1 26.8 %copy-start.27 = (pred[4]{0:T(512)(128)(4,1)}, pred[4]{0:T(512)(128)(4,1)S(1)}, u32[]{:S(2)}) copy-start(pred[4]{0:T(512)(128)(4,1)S(1)} %get-tuple-element.442) | copy-start | bytes 16
  68.0 7.8 copy-start.12
  69.0 8.3 copy-start.13
  70.8 7.3 copy-start.14
  70.8 8.2 copy-start.15
  70.8 8.1 copy-start.43
  353.2 18.0 %collective-permute-start.7 = (f32[1,4,3,4096]{3,2,1,0:T(4,128)}, f32[1,4,3,4096]{3,2,1,0:T(4,128)}, u32[]{:S(2)}, u32[]{:S(2)}) collective-permute-start(f32[1,4,3,4096]{3,2,1,0:T(4,128)} %get-tuple-element.552), channel_id=1, source_target_pairs={{1,0},{2,1},{3,2},{4,3},{5,4},{6,5},{7,6},{8,7},{9,8},{10,9},{11,1... | collective-permute-start | bytes 589832 | tf_op jit(solution)/shard_map/ppermute | solution.py:18
  356.2 16.1 %collective-permute-start.6 = (f32[1,4,3,4096]{3,2,1,0:T(4,128)}, f32[1,4,3,4096]{3,2,1,0:T(4,128)S(1)}, u32[]{:S(2)}, u32[]{:S(2)}) collective-permute-start(f32[1,4,3,4096]{3,2,1,0:T(4,128)} %get-tuple-element.551), channel_id=1, source_target_pairs={{0,1},{1,2},{2,3},{3,4},{4,5},{5,6},{6,7},{7,8},{8,9},{9,10},{10,1... | collective-permute-start | bytes 589832 | tf_op jit(solution)/shard_map/ppermute | solution.py:15
  360.1 12.4 %collective-permute-start.5 = (f32[1,4,3,4096]{3,2,1,0:T(4,128)}, f32[1,4,3,4096]{3,2,1,0:T(4,128)S(1)}, u32[]{:S(2)}, u32[]{:S(2)}) collective-permute-start(f32[1,4,3,4096]{3,2,1,0:T(4,128)} %get-tuple-element.550), channel_id=1, source_target_pairs={{16,0},{32,16},{48,32},{64,48},{80,64},{96,80},{112,96},{17,1},{33... | collective-permute-start | bytes 589832 | tf_op jit(solution)/shard_map/ppermute | solution.py:18
  361.4 15.6 %collective-permute-start.4 = (f32[1,4,3,4096]{3,2,1,0:T(4,128)}, f32[1,4,3,4096]{3,2,1,0:T(4,128)}, u32[]{:S(2)}, u32[]{:S(2)}) collective-permute-start(f32[1,4,3,4096]{3,2,1,0:T(4,128)} %get-tuple-element.549), channel_id=1, source_target_pairs={{0,16},{16,32},{32,48},{48,64},{64,80},{80,96},{96,112},{1,17},{17... | collective-permute-start | bytes 589832 | tf_op jit(solution)/shard_map/ppermute | solution.py:15
  660.1 17.2 %collective-permute-start.11 = (f32[1,4,3,4096]{3,2,1,0:T(4,128)}, f32[1,4,3,4096]{3,2,1,0:T(4,128)}, u32[]{:S(2)}, u32[]{:S(2)}) collective-permute-start(f32[1,4,3,4096]{3,2,1,0:T(4,128)} %get-tuple-element.536), channel_id=1, source_target_pairs={{1,0},{2,1},{3,2},{4,3},{5,4},{6,5},{7,6},{8,7},{9,8},{10,9},{11,1... | collective-permute-start | bytes 589832 | tf_op jit(solution)/shard_map/ppermute | solution.py:18
  663.0 15.3 %collective-permute-start.10 = (f32[1,4,3,4096]{3,2,1,0:T(4,128)}, f32[1,4,3,4096]{3,2,1,0:T(4,128)S(1)}, u32[]{:S(2)}, u32[]{:S(2)}) collective-permute-start(f32[1,4,3,4096]{3,2,1,0:T(4,128)} %get-tuple-element.535), channel_id=1, source_target_pairs={{0,1},{1,2},{2,3},{3,4},{4,5},{5,6},{6,7},{7,8},{8,9},{9,10},{10,1... | collective-permute-start | bytes 589832 | tf_op jit(solution)/shard_map/ppermute | solution.py:15
  666.9 11.5 %collective-permute-start.9 = (f32[1,4,3,4096]{3,2,1,0:T(4,128)}, f32[1,4,3,4096]{3,2,1,0:T(4,128)S(1)}, u32[]{:S(2)}, u32[]{:S(2)}) collective-permute-start(f32[1,4,3,4096]{3,2,1,0:T(4,128)} %get-tuple-element.534), channel_id=1, source_target_pairs={{16,0},{32,16},{48,32},{64,48},{80,64},{96,80},{112,96},{17,1},{33... | collective-permute-start | bytes 589832 | tf_op jit(solution)/shard_map/ppermute | solution.py:18
  668.2 15.0 %collective-permute-start.8 = (f32[1,4,3,4096]{3,2,1,0:T(4,128)}, f32[1,4,3,4096]{3,2,1,0:T(4,128)}, u32[]{:S(2)}, u32[]{:S(2)}) collective-permute-start(f32[1,4,3,4096]{3,2,1,0:T(4,128)} %get-tuple-element.533), channel_id=1, source_target_pairs={{0,16},{16,32},{32,48},{48,64},{64,80},{80,96},{96,112},{1,17},{17... | collective-permute-start | bytes 589832 | tf_op jit(solution)/shard_map/ppermute | solution.py:15
  692.8 226.0 %copy-start.60 = (pred[4]{0:T(512)(128)(4,1)S(1)}, pred[4]{0:T(512)(128)(4,1)}, u32[]{:S(2)}) copy-start(pred[4]{0:T(512)(128)(4,1)} %iota_compare_fusion) | copy-start | bytes 16
  (76 other events, 280.9 us)
where the time goes:
time: 940 us; the launch traced here: 928 us
  other arithmetic  507 us (54%)
  local copies, waits for them, and re-layouts  374 us (40%)
  starting transfers between devices  32.1 us (3%)
  loops' own time  12.6 us (1%)
    sub x12, other arithmetic, tile_rate(): jnp.sqrt(squares.reshape(edge_size, edge_size * edge_size)) - 1.0  266 us
    select_n x12, other arithmetic, upwind_square(): return jnp.where(sign_part > 0.0, outward, inward)  75.5 us
    unnamed x147, local copies, waits for them, and re-layouts  53 us
    concatenate x12, other arithmetic, tile_rate(): padded = jnp.concatenate([low_z, cube_view, high_z], axis=2)  40.4 us
    slice x3, local copies, waits for them, and re-layouts, all_layers(): cube_view[:, :, edge_size - 3:]  39.6 us
    while x72, local copies, waits for them, and re-layouts  33 us
    dynamic_update_slice x12, other arithmetic, one_tile(): lax.dynamic_update_index_in_dim(totals, tile_rate(tile_flat, halo_layers,...  27.8 us
    reshape x12, local copies, waits for them, and re-layouts, tile_rate(): upwind_square(minus_side, plus_side, sign_tile)  26 us
  transfers between devices with their start and end apart: 12, of which 0 were waited for; matrix products, arithmetic and copies ran while one was open for 5% of the time, Pallas kernels for 0%

commit v1 on v0

v1 whole, which is shorter than its diff:
```python
import functools

import jax
import jax.numpy as jnp
from jax import lax
from jax.experimental import pallas as pl
from jax.experimental.pallas import tpu as pltpu
from jax.sharding import PartitionSpec as P

weno_eps = 1e-06
pseudo_step = 0.3
scale_s = pseudo_step / 3.0

SLOTS = 4
EDGE = 64
FACE = SLOTS * 3 * 4


def rcp(x):
    return pl.reciprocal(x, approx=True)


def aligned(start, count=8):
    return pl.ds(pl.multiple_of(start, 8), count)


def column(load, load_s, emit, n):
    kept = {}

    def memo(name, p, make):
        key = (name, p)
        if key not in kept:
            kept[key] = make()
        return kept[key]

    U = lambda p: memo("u", p, lambda: load(p))
    D = lambda p: memo("d", p, lambda: U(p + 1) - U(p))
    E = lambda p: memo("e", p, lambda: D(p) - D(p - 1))
    EH = lambda p: memo("eh", p, lambda: E(p) * 0.5)
    FH = lambda p: memo("fh", p, lambda: EH(p + 1) - EH(p))
    GH = lambda p: memo("gh", p, lambda: FH(p) - FH(p - 1))
    G15 = lambda p: memo("g15", p, lambda: GH(p) * 1.5)
    FF = lambda p: memo("ff", p, lambda: (FH(p) * FH(p)) * (8.0 / 3.0) + 0.5 * weno_eps)
    SQ = lambda p: memo("sq", p, lambda: E(p) * E(p))
    PP = lambda p: memo("pp", p, lambda: E(p) * EH(p + 1))
    LOW = lambda p: memo("low", p, lambda: FF(p) - PP(p))

    def face(j):
        def make():
            ra = rcp(LOW(j - 2) + SQ(j - 1))
            rb = rcp(FF(j - 1) + PP(j - 1))
            c = LOW(j) + SQ(j)
            xr = c * ra
            yr = c * rb
            x = xr * xr
            y = (yr * yr) * 3.0
            w = x * 0.5 + y
            a = x * GH(j - 1)
            minus = (a + G15(j)) * rcp(w + 1.5)
            plus = (GH(j) + a * 1.5) * rcp((w + 0.5) + x)
            return minus, plus

        return memo("face", j, make)

    for i in range(n):
        qm = face(i)[0]
        qp = face(i + 1)[1]
        t = (U(i + 1) - U(i - 1)) + (D(i - 1) + EH(i - 1))
        s = load_s(i)
        w = jnp.maximum(jnp.maximum(s * (t - qm), s * ((GH(i) - t) - qp)), 0.0)
        emit(i, w * w)


def w_row(t, ib, j):
    return ((t * 8 + ib) * 32 + j) * 8


def v_block(t, block, k):
    return (t * 4 + block) * EDGE + k


def face_block(side, t, h, c):
    return ((side * SLOTS + t) * 3 + h) * 4 + c


def one_if_none(n):
    return jnp.maximum(-n, 0)


def one_if_far(n):
    return jnp.minimum(jnp.maximum(n - (SLOTS - 1), 0), 1)


def kernel(
    level_ref, nb_ref, out_ref,
    wa, wb, wc, s_ref, v_ref, sv_ref, gx_ref, gz_ref, gva, gvb,
    x_faces0, x_faces1, x_faces2, y_faces0, y_faces1, y_faces2, send_sem, recv_sem,
):
    v_rows = v_ref.reshape(SLOTS * 4 * EDGE * 8, 128)
    gx, gy = lax.axis_index("gx"), lax.axis_index("gy")
    n_gx, n_gy = lax.axis_size("gx"), lax.axis_size("gy")
    x_low, x_high = lax.rem(gx + n_gx - 1, n_gx), lax.rem(gx + 1, n_gx)
    y_low, y_high = lax.rem(gy + n_gy - 1, n_gy), lax.rem(gy + 1, n_gy)
    lanes_low = lax.broadcasted_iota(jnp.int32, (8, 128), 1) < 64

    def roll(x):
        return pltpu.roll(x, 64, axis=1)

    barrier = pltpu.get_barrier_semaphore()
    around = ((x_low, gy), (x_high, gy), (gx, y_low), (gx, y_high))
    for device in around:
        pl.semaphore_signal(barrier, inc=1, device_id=device, device_id_type=pl.DeviceIdType.MESH)

    def to_v(values, t, ib, half):
        turned = jnp.concatenate(values, axis=0).T
        for jh in range(2):
            line = lax.rem(ib, 2) * 4 + half * 2 + jh
            for m in range(8):
                r = jh * 64 + 8 * m
                start = v_block(t, ib // 2, 8 * m) * 8 + line
                v_rows[pl.ds(start, 8, stride=8), :] = turned[r:r + 8]

    def enter(it, carry):
        t, ib = it // 8, lax.rem(it, 8)
        rows = aligned(ib * 8)
        values = []
        for m in range(16):
            a = level_ref[t, rows, m * 128:(m + 1) * 128]
            b = level_ref[t, rows, (m + 16) * 128:(m + 17) * 128]
            values.append(jnp.where(lanes_low, a, roll(b)))
            values.append(jnp.where(lanes_low, roll(a), b))
        for j in range(32):
            u = values[j]
            wa[aligned(w_row(t, ib, j)), :] = u
            s_ref[aligned(w_row(t, ib, j)), :] = (u * scale_s) * lax.rsqrt(u * u + 1.0)
        for half in range(2):
            to_v(values[16 * half:16 * half + 16], t, ib, half)
        return carry

    lax.fori_loop(0, 32, enter, 0)

    def turned_sign(it, carry):
        for k in range(64):
            u = v_ref[it * 64 + k]
            sv_ref[it * 64 + k] = (u * scale_s) * lax.rsqrt(u * u + 1.0)
        return carry

    lax.fori_loop(0, 16, turned_sign, 0)
    gvb[...] = jnp.zeros_like(gvb)
    pl.semaphore_wait(barrier, 4)

    def section(stage, u_ref, n_ref, xf, yf):
        def pack(t, carry):
            for side in range(2):
                for h in range(3):
                    i = h if side == 0 else 61 + h
                    for c in range(4):
                        rows = pl.ds(w_row(t, i // 8, 8 * c) + i % 8, 8, stride=8)
                        xf[face_block(side, t, h, c)] = u_ref[rows, :]
                    for q in range(4):
                        j = h if side == 0 else 29 + h
                        even = u_ref[aligned(w_row(t, 2 * q, j)), :]
                        odd = u_ref[aligned(w_row(t, 2 * q + 1, j)), :]
                        if side == 0:
                            both = jnp.where(lanes_low, even, roll(odd))
                        else:
                            both = jnp.where(lanes_low, roll(even), odd)
                        yf[face_block(side, t, h, q)] = both
            return carry

        lax.fori_loop(0, 4, pack, 0)
        low, high, below, above = (pl.ds(part * FACE, FACE) for part in range(4))
        plan = (
            (xf, high, below, (x_high, gy)), (xf, low, above, (x_low, gy)),
            (yf, high, below, (gx, y_high)), (yf, low, above, (gx, y_low)),
        )
        copies = []
        for f, (table, source, target, device) in enumerate(plan):
            copy = pltpu.make_async_remote_copy(
                src_ref=table.at[source], dst_ref=table.at[target], send_sem=send_sem.at[stage, f],
                recv_sem=recv_sem.at[stage, f], device_id=device, device_id_type=pl.DeviceIdType.MESH,
            )
            copy.start()
            copies.append(copy)

        def z_back(source, it):
            for pair in range(4):
                parts = [
                    source[pl.ds(64 * m + 2 * pair + jh, 8, stride=8), :] for jh in range(2) for m in range(8)
                ]
                gz_ref[aligned(512 + it * 512 + pair * 128, 128), :] = jnp.concatenate(parts, axis=0).T

        def z_stream(it, target):
            t, block = it // 4, lax.rem(it, 4)
            base = v_block(t, block, 0)

            def layer(n, own, other):
                none = one_if_none(n)
                return none * (t * 256 + own) + (1 - none) * (n * 256 + other) + block * EDGE

            n_low, n_high = nb_ref[t, 4], nb_ref[t, 5]

            def load(p):
                if p < 0:
                    return v_ref[layer(n_low, 0, 64 + p)]
                if p >= 64:
                    return v_ref[layer(n_high, 63, p - 64)]
                return v_ref[base + p]

            def emit(i, squares):
                target[pl.ds(i * 8, 8), :] = squares

            column(load, lambda i: sv_ref[base + i], emit, 64)

        def z_pair(n, carry):
            z_back(gvb, 2 * n - 1)
            z_stream(2 * n, gva)
            z_back(gva, 2 * n)
            z_stream(2 * n + 1, gvb)
            return carry

        lax.fori_loop(0, 8, z_pair, 0)
        z_back(gvb, 15)

        for copy in copies:
            copy.wait()

        def face_source(t, f, table):
            n = nb_ref[t, f]
            own_side, other_side = (0, 1) if f % 2 == 0 else (1, 0)
            outer = 0 if f % 2 == 0 else 2
            none, far = one_if_none(n), one_if_far(n)
            own = none * face_block(own_side, t, outer, 0)
            near = (1 - none) * (1 - far) * face_block(other_side, n, 0, 0)
            away = far * ((2 + f % 2) * FACE + (n - SLOTS) * 12)

            def get(h, c):
                return table[own + near + away + (1 - none) * (4 * h) + c]

            return get

        def x_stream(it, carry):
            t, c = it // 4, lax.rem(it, 4)
            get_low = face_source(t, 0, xf)
            get_high = face_source(t, 1, xf)

            def rows(i):
                return pl.ds(w_row(t, i // 8, 8 * c) + i % 8, 8, stride=8)

            def load(p):
                if p < 0:
                    return get_low(p + 3, c)
                if p >= 64:
                    return get_high(p - 64, c)
                return u_ref[rows(p), :]

            def emit(i, squares):
                gx_ref[rows(i), :] = squares

            column(load, lambda i: s_ref[rows(i), :], emit, 64)
            return carry

        lax.fori_loop(0, 16, x_stream, 0)

        def y_stream(t, q, parity, lows, highs):
            ib = 2 * q + parity
            base = w_row(t, ib, 0)
            new = {}

            def load(p):
                if p < 0:
                    h = p + 3
                    halo = lows[h] if parity == 0 else roll(lows[h])
                    return jnp.where(lanes_low, halo, roll(u_ref[aligned(base + (29 + h) * 8), :]))
                if p >= 32:
                    h = p - 32
                    halo = roll(highs[h]) if parity == 0 else highs[h]
                    return jnp.where(lanes_low, roll(u_ref[aligned(base + h * 8), :]), halo)
                return u_ref[aligned(base + p * 8), :]

            def emit(j, squares):
                rows = aligned(base + j * 8)
                total = (squares + gx_ref[rows, :]) + gz_ref[aligned(512 + base + j * 8), :]
                size = total * lax.rsqrt(jnp.maximum(total, 1e-35))
                s = s_ref[rows, :]
                u = u_ref[rows, :]
                moved = u + s * 3.0
                moved = jnp.where(s > 0.0, moved - size, moved + size)
                if stage == 1:
                    moved = 0.75 * wa[rows, :] + 0.25 * moved
                elif stage == 2:
                    moved = (1.0 / 3.0) * wa[rows, :] + (2.0 / 3.0) * moved
                if stage < 2:
                    n_ref[rows, :] = moved
                new[j] = moved
                if stage == 2 and j % 2 == 1:
                    a, b = new[j - 1], moved
                    m = j // 2
                    orow = aligned(ib * 8)
                    out_ref[t, orow, m * 128:(m + 1) * 128] = jnp.where(lanes_low, a, roll(b))
                    out_ref[t, orow, (m + 16) * 128:(m + 17) * 128] = jnp.where(lanes_low, roll(a), b)

            column(load, lambda j: s_ref[aligned(base + j * 8), :], emit, 32)
            return [new[j] for j in range(32)]

        def y_pair(it, carry):
            t, q = it // 4, lax.rem(it, 4)
            get_low = face_source(t, 2, yf)
            get_high = face_source(t, 3, yf)
            lows = [get_low(h, q) for h in range(3)]
            highs = [get_high(h, q) for h in range(3)]
            for parity in range(2):
                values = y_stream(t, q, parity, lows, highs)
                if stage < 2:
                    for half in range(2):
                        to_v(values[16 * half:16 * half + 16], t, 2 * q + parity, half)
            return carry

        lax.fori_loop(0, 16, y_pair, 0)

    section(0, wa, wb, x_faces0, y_faces0)
    section(1, wb, wc, x_faces1, y_faces1)
    section(2, wc, None, x_faces2, y_faces2)


def local(level_set, tile_count, neighbours):
    rows = lambda count: pltpu.VMEM((count, 128), jnp.float32)
    blocks = lambda count: pltpu.VMEM((count, 8, 128), jnp.float32)
    whole = SLOTS * EDGE ** 3 // 128
    scratch = [rows(whole), rows(whole), rows(whole), rows(whole), blocks(whole // 8), blocks(whole // 8),
               rows(whole), rows(whole + 512), rows(512), rows(512)]
    scratch += [blocks(4 * FACE) for _ in range(6)]
    scratch += [pltpu.SemaphoreType.DMA((3, 4)), pltpu.SemaphoreType.DMA((3, 4))]
    cells = SLOTS * EDGE ** 3
    moved = pl.pallas_call(
        kernel,
        out_shape=jax.ShapeDtypeStruct(level_set.shape, jnp.float32),
        in_specs=[
            pl.BlockSpec(memory_space=pltpu.VMEM),
            pl.BlockSpec(memory_space=pltpu.SMEM),
        ],
        out_specs=pl.BlockSpec(memory_space=pltpu.VMEM),
        scratch_shapes=scratch,
        compiler_params=pltpu.CompilerParams(
            collective_id=0, has_side_effects=True, vmem_limit_bytes=60 * 2 ** 20
        ),
        cost_estimate=pl.CostEstimate(flops=cells * 3 * 150, bytes_accessed=cells * 8, transcendentals=cells * 3),
    )(level_set, neighbours)
    live = jnp.arange(SLOTS, dtype=jnp.int32) < tile_count[0]
    return jnp.where(live[:, None, None], moved, 0.0)


def solution(mesh):
    placed = (P(("gx", "gy"), None, None), P(("gx", "gy")), P(("gx", "gy"), None))
    return jax.shard_map(
        local, mesh=mesh, in_specs=placed, out_specs=P(("gx", "gy"), None, None), check_vma=False
    )
```

time: 940 us -> 95.8 us (0.10)
  the two profiles are of different devices: /device:TPU:2 before, /device:TPU:1 now
where the time goes in v1:
time: 95.8 us; the launch traced here: 95.6 us
  Pallas kernels  90.1 us (94%)
  other arithmetic  4.83 us (5%)
    pallas_call x1, Pallas kernels, local(): pl.pallas_call(kernel, out_shape=jax.ShapeDtypeStruct(level_set.shape, jn...  90.1 us
    select_n x1, other arithmetic, local(): return jnp.where(live[:, None, None], moved, 0.0)  4.82 us

profile of v1, /device:TPU:1, one launch (start us, length us, event | category | flops | bytes accessed | tf_op | source)
XLA Modules:
  0.0 95.6 jit_solution(8219983973081564286)
XLA Ops:
  0.7 90.1 %shard_map.37 = f32[4,64,4096]{2,1,0:T(8,128)} custom-call(f32[4,64,4096]{2,1,0:T(8,128)} %level_ref.1, s32[4,6]{1,0:T(4,128)} %nb_ref.1), custom_call_target="tpu_custom_call" | custom-call | flops 471859200 | bytes 8388608 | tf_op jit(solution)/shard_map/pallas_call | solution.py:335
  90.8 4.8 %broadcast_select_fusion = f32[4,64,4096]{2,1,0:T(8,128)} fusion(f32[4,64,4096]{2,1,0:T(8,128)} %shard_map.37, pred[4]{0:T(512)(128)(4,1)S(1)} %iota_compare_fusion), kind=kLoop, calls=%fused_computation | loop fusion | flops 1048576 | bytes 8388612 | tf_op jit(solution)/shard_map/jit(_where)/select_n | solution.py:350
  (1 shorter events, 0.0 us)

commit v2 on v1

--- a/solution.py
+++ b/solution.py
@@ -24,7 +24,7 @@
     return pl.ds(pl.multiple_of(start, 8), count)
 
 
-def column(load, load_s, emit, n):
+def column(load, load_s, emit, n, between=None):
     kept = {}
 
     def memo(name, p, make):
@@ -69,6 +69,8 @@
         s = load_s(i)
         w = jnp.maximum(jnp.maximum(s * (t - qm), s * ((GH(i) - t) - qp)), 0.0)
         emit(i, w * w)
+        if between is not None:
+            between(i)
 
 
 def w_row(t, ib, j):
@@ -93,10 +95,15 @@
 
 def kernel(
     level_ref, nb_ref, out_ref,
-    wa, wb, wc, s_ref, v_ref, sv_ref, gx_ref, gz_ref, gva, gvb,
-    x_faces0, x_faces1, x_faces2, y_faces0, y_faces1, y_faces2, send_sem, recv_sem,
+    wa, wb, wc, s_ref, ux_ref, sx_ref, v_ref, sv_ref, gx_ref, gz_ref, gva, gvb,
+    x_faces0, x_faces1, x_faces2, y_faces0, y_faces1, y_faces2, send_sem, recv_sem, load_sem,
 ):
     v_rows = v_ref.reshape(SLOTS * 4 * EDGE * 8, 128)
+    ux_rows = ux_ref.reshape(SLOTS * 4 * EDGE * 8, 128)
+    sx_rows = sx_ref.reshape(SLOTS * 4 * EDGE * 8, 128)
+
+    def x_rows(t, ib, j):
+        return pl.ds(v_block(t, j // 8, ib * 8) * 8 + j % 8, 8, stride=8)
     gx, gy = lax.axis_index("gx"), lax.axis_index("gy")
     n_gx, n_gy = lax.axis_size("gx"), lax.axis_size("gy")
     x_low, x_high = lax.rem(gx + n_gx - 1, n_gx), lax.rem(gx + 1, n_gx)
@@ -105,6 +112,11 @@
 
     def roll(x):
         return pltpu.roll(x, 64, axis=1)
+
+    tile_rows = [pl.ds(t * 2048, 2048) for t in range(SLOTS)]
+    loads = [pltpu.make_async_copy(level_ref.at[r], wc.at[r], load_sem.at[t]) for t, r in enumerate(tile_rows)]
+    for load in loads:
+        load.start()
 
     barrier = pltpu.get_barrier_semaphore()
     around = ((x_low, gy), (x_high, gy), (gx, y_low), (gx, y_high))
@@ -120,24 +132,31 @@
                 start = v_block(t, ib // 2, 8 * m) * 8 + line
                 v_rows[pl.ds(start, 8, stride=8), :] = turned[r:r + 8]
 
-    def enter(it, carry):
-        t, ib = it // 8, lax.rem(it, 8)
-        rows = aligned(ib * 8)
+    def enter_block(t, ib):
         values = []
         for m in range(16):
-            a = level_ref[t, rows, m * 128:(m + 1) * 128]
-            b = level_ref[t, rows, (m + 16) * 128:(m + 17) * 128]
+            a = wc[aligned(w_row(t, ib, m)), :]
+            b = wc[aligned(w_row(t, ib, m + 16)), :]
             values.append(jnp.where(lanes_low, a, roll(b)))
             values.append(jnp.where(lanes_low, roll(a), b))
         for j in range(32):
             u = values[j]
             wa[aligned(w_row(t, ib, j)), :] = u
-            s_ref[aligned(w_row(t, ib, j)), :] = (u * scale_s) * lax.rsqrt(u * u + 1.0)
+            s = (u * scale_s) * lax.rsqrt(u * u + 1.0)
+            s_ref[aligned(w_row(t, ib, j)), :] = s
+            ux_rows[x_rows(t, ib, j), :] = u
+            sx_rows[x_rows(t, ib, j), :] = s
         for half in range(2):
             to_v(values[16 * half:16 * half + 16], t, ib, half)
-        return carry
-
-    lax.fori_loop(0, 32, enter, 0)
+
+    for t in range(SLOTS):
+        def enter(q, carry, t=t):
+            for e in range(2):
+                enter_block(t, 2 * q + e)
+            return carry
+
+        loads[t].wait()
+        lax.fori_loop(0, 4, enter, 0)
 
     def turned_sign(it, carry):
         for k in range(64):
@@ -155,8 +174,7 @@
                 for h in range(3):
                     i = h if side == 0 else 61 + h
                     for c in range(4):
-                        rows = pl.ds(w_row(t, i // 8, 8 * c) + i % 8, 8, stride=8)
-                        xf[face_block(side, t, h, c)] = u_ref[rows, :]
+                        xf[face_block(side, t, h, c)] = ux_ref[v_block(t, c, i)]
                     for q in range(4):
                         j = h if side == 0 else 29 + h
                         even = u_ref[aligned(w_row(t, 2 * q, j)), :]
@@ -183,14 +201,11 @@
             copy.start()
             copies.append(copy)
 
-        def z_back(source, it):
-            for pair in range(4):
-                parts = [
-                    source[pl.ds(64 * m + 2 * pair + jh, 8, stride=8), :] for jh in range(2) for m in range(8)
-                ]
-                gz_ref[aligned(512 + it * 512 + pair * 128, 128), :] = jnp.concatenate(parts, axis=0).T
-
-        def z_stream(it, target):
+        def z_back(source, it, pair):
+            parts = [source[pl.ds((8 * m + 2 * pair + jh) * 8, 8), :] for jh in range(2) for m in range(8)]
+            gz_ref[aligned(512 + it * 512 + pair * 128, 128), :] = jnp.concatenate(parts, axis=0).T
+
+        def z_stream(it, target, before):
             t, block = it // 4, lax.rem(it, 4)
             base = v_block(t, block, 0)
 
@@ -208,19 +223,22 @@
                 return v_ref[base + p]
 
             def emit(i, squares):
-                target[pl.ds(i * 8, 8), :] = squares
-
-            column(load, lambda i: sv_ref[base + i], emit, 64)
+                target[pl.ds((i // 8) * 64 + i % 8, 8, stride=8), :] = squares
+
+            def between(i):
+                if i % 16 == 4:
+                    z_back(before, it - 1, i // 16)
+
+            column(load, lambda i: sv_ref[base + i], emit, 64, between)
 
         def z_pair(n, carry):
-            z_back(gvb, 2 * n - 1)
-            z_stream(2 * n, gva)
-            z_back(gva, 2 * n)
-            z_stream(2 * n + 1, gvb)
+            z_stream(2 * n, gva, gvb)
+            z_stream(2 * n + 1, gvb, gva)
             return carry
 
         lax.fori_loop(0, 8, z_pair, 0)
-        z_back(gvb, 15)
+        for pair in range(4):
+            z_back(gvb, 15, pair)
 
         for copy in copies:
             copy.wait()
@@ -239,30 +257,25 @@
 
             return get
 
-        def x_stream(it, carry):
-            t, c = it // 4, lax.rem(it, 4)
+        def x_stream(t, c):
             get_low = face_source(t, 0, xf)
             get_high = face_source(t, 1, xf)
 
-            def rows(i):
-                return pl.ds(w_row(t, i // 8, 8 * c) + i % 8, 8, stride=8)
+            base = v_block(t, c, 0)
 
             def load(p):
                 if p < 0:
                     return get_low(p + 3, c)
                 if p >= 64:
                     return get_high(p - 64, c)
-                return u_ref[rows(p), :]
+                return ux_ref[base + p]
 
             def emit(i, squares):
-                gx_ref[rows(i), :] = squares
-
-            column(load, lambda i: s_ref[rows(i), :], emit, 64)
-            return carry
-
-        lax.fori_loop(0, 16, x_stream, 0)
-
-        def y_stream(t, q, parity, lows, highs):
+                gx_ref[pl.ds(w_row(0, i // 8, 8 * c) + i % 8, 8, stride=8), :] = squares
+
+            column(load, lambda i: sx_ref[base + i], emit, 64)
+
+        def y_stream(t, q, parity, lows, highs, between):
             ib = 2 * q + parity
             base = w_row(t, ib, 0)
             new = {}
@@ -280,7 +293,7 @@
 
             def emit(j, squares):
                 rows = aligned(base + j * 8)
-                total = (squares + gx_ref[rows, :]) + gz_ref[aligned(512 + base + j * 8), :]
+                total = (squares + gx_ref[aligned(w_row(0, ib, j)), :]) + gz_ref[aligned(512 + base + j * 8), :]
                 size = total * lax.rsqrt(jnp.maximum(total, 1e-35))
                 s = s_ref[rows, :]
                 u = u_ref[rows, :]
@@ -292,6 +305,7 @@
                     moved = (1.0 / 3.0) * wa[rows, :] + (2.0 / 3.0) * moved
                 if stage < 2:
                     n_ref[rows, :] = moved
+                    ux_rows[x_rows(t, ib, j), :] = moved
                 new[j] = moved
                 if stage == 2 and j % 2 == 1:
                     a, b = new[j - 1], moved
@@ -300,23 +314,31 @@
                     out_ref[t, orow, m * 128:(m + 1) * 128] = jnp.where(lanes_low, a, roll(b))
                     out_ref[t, orow, (m + 16) * 128:(m + 17) * 128] = jnp.where(lanes_low, roll(a), b)
 
-            column(load, lambda j: s_ref[aligned(base + j * 8), :], emit, 32)
-            return [new[j] for j in range(32)]
-
-        def y_pair(it, carry):
-            t, q = it // 4, lax.rem(it, 4)
+            column(load, lambda j: s_ref[aligned(base + j * 8), :], emit, 32, between)
+
+        def y_pair(t, q):
+            it = t * 4 + q
             get_low = face_source(t, 2, yf)
             get_high = face_source(t, 3, yf)
             lows = [get_low(h, q) for h in range(3)]
             highs = [get_high(h, q) for h in range(3)]
-            for parity in range(2):
-                values = y_stream(t, q, parity, lows, highs)
-                if stage < 2:
-                    for half in range(2):
-                        to_v(values[16 * half:16 * half + 16], t, 2 * q + parity, half)
+            before = jnp.maximum(it - 1, 0)
+            y_stream(t, q, 0, lows, highs, functools.partial(turn, before // 4, 2 * lax.rem(before, 4) + 1))
+            y_stream(t, q, 1, lows, highs, functools.partial(turn, t, 2 * q))
+
+        def turn(t, ib, j):
+            if stage < 2 and j % 16 == 4:
+                half = j // 16
+                to_v([n_ref[aligned(w_row(t, ib, 16 * half + k)), :] for k in range(16)], t, ib, half)
+
+        def tile(t, carry):
+            lax.fori_loop(0, 4, lambda c, kept: (x_stream(t, c), kept)[1], 0)
+            lax.fori_loop(0, 4, lambda q, kept: (y_pair(t, q), kept)[1], 0)
             return carry
 
-        lax.fori_loop(0, 16, y_pair, 0)
+        lax.fori_loop(0, SLOTS, tile, 0)
+        for j in (4, 20):
+            turn(3, 7, j)
 
     section(0, wa, wb, x_faces0, y_faces0)
     section(1, wb, wc, x_faces1, y_faces1)
@@ -328,24 +350,26 @@
     blocks = lambda count: pltpu.VMEM((count, 8, 128), jnp.float32)
     whole = SLOTS * EDGE ** 3 // 128
     scratch = [rows(whole), rows(whole), rows(whole), rows(whole), blocks(whole // 8), blocks(whole // 8),
-               rows(whole), rows(whole + 512), rows(512), rows(512)]
+               blocks(whole // 8), blocks(whole // 8),
+               rows(whole // SLOTS), rows(whole + 512), rows(512), rows(512)]
     scratch += [blocks(4 * FACE) for _ in range(6)]
-    scratch += [pltpu.SemaphoreType.DMA((3, 4)), pltpu.SemaphoreType.DMA((3, 4))]
+    scratch += [pltpu.SemaphoreType.DMA((3, 4)), pltpu.SemaphoreType.DMA((3, 4)), pltpu.SemaphoreType.DMA((SLOTS,))]
     cells = SLOTS * EDGE ** 3
+    blocked = level_set.reshape(SLOTS, 8, 8, 32, 128).transpose(0, 1, 3, 2, 4).reshape(whole, 128)
     moved = pl.pallas_call(
         kernel,
         out_shape=jax.ShapeDtypeStruct(level_set.shape, jnp.float32),
         in_specs=[
-            pl.BlockSpec(memory_space=pltpu.VMEM),
+            pl.BlockSpec(memory_space=pl.ANY),
             pl.BlockSpec(memory_space=pltpu.SMEM),
         ],
         out_specs=pl.BlockSpec(memory_space=pltpu.VMEM),
         scratch_shapes=scratch,
         compiler_params=pltpu.CompilerParams(
-            collective_id=0, has_side_effects=True, vmem_limit_bytes=60 * 2 ** 20
+            collective_id=0, has_side_effects=True, vmem_limit_bytes=47 * 2 ** 20
         ),
         cost_estimate=pl.CostEstimate(flops=cells * 3 * 150, bytes_accessed=cells * 8, transcendentals=cells * 3),
-    )(level_set, neighbours)
+    )(blocked, neighbours)
     live = jnp.arange(SLOTS, dtype=jnp.int32) < tile_count[0]
     return jnp.where(live[:, None, None], moved, 0.0)
 

time: 95.8 us -> 86.4 us (0.902)
  Pallas kernels: 90.1 us -> 82.5 us
  other arithmetic: 4.83 us -> 2.49 us
    pallas_call x1, Pallas kernels: 90.1 us -> 82.5 us  [local(): pl.pallas_call(kernel, out_shape=jax.ShapeDtypeStruct(level_set.shape, jn...]
    select_n x1, other arithmetic: 4.82 us -> 2.49 us  [local(): return jnp.where(live[:, None, None], moved, 0.0)]
where the time goes in v2:
time: 86.4 us; the launch traced here: 86.3 us
  Pallas kernels  82.5 us (95%)
  other arithmetic  2.49 us (3%)
    pallas_call x1, Pallas kernels, local(): pl.pallas_call(kernel, out_shape=jax.ShapeDtypeStruct(level_set.shape, jn...  82.5 us
    select_n x1, other arithmetic, local(): return jnp.where(live[:, None, None], moved, 0.0)  2.49 us

profile of v2, /device:TPU:1, one launch (start us, length us, event | category | flops | bytes accessed | tf_op | source)
XLA Modules:
  0.0 86.3 jit_solution(13470824088286843221)
XLA Ops:
  0.7 0.0 copy-start
  0.7 0.7 copy-done
  1.3 82.5 %shard_map.37 = f32[4,64,4096]{2,1,0:T(8,128)S(1)} custom-call(f32[8192,128]{1,0:T(8,128)} %bitcast.7, s32[4,6]{1,0:T(4,128)S(1)} %copy-done), custom_call_target="tpu_custom_call" | custom-call | flops 471859200 | bytes 8388608 | tf_op jit(solution)/shard_map/pallas_call | solution.py:359
  83.8 2.5 %broadcast_select_fusion = f32[4,64,4096]{2,1,0:T(8,128)} fusion(f32[4,64,4096]{2,1,0:T(8,128)S(1)} %shard_map.37, pred[4]{0:T(512)(128)(4,1)S(1)} %iota_compare_fusion), kind=kLoop, calls=%fused_computation | loop fusion | flops 1048576 | bytes 8388612 | tf_op jit(solution)/shard_map/jit(_where)/select_n | solution.py:374
  (1 shorter events, 0.0 us)
Async XLA Ops:
  0.7 0.7 copy-start

commit v3 on v2

--- a/solution.py
+++ b/solution.py
@@ -68,7 +68,7 @@
         t = (U(i + 1) - U(i - 1)) + (D(i - 1) + EH(i - 1))
         s = load_s(i)
         w = jnp.maximum(jnp.maximum(s * (t - qm), s * ((GH(i) - t) - qp)), 0.0)
-        emit(i, w * w)
+        emit(i, w * w, U(i), s)
         if between is not None:
             between(i)
 
@@ -222,7 +222,7 @@
                     return v_ref[layer(n_high, 63, p - 64)]
                 return v_ref[base + p]
 
-            def emit(i, squares):
+            def emit(i, squares, u, s):
                 target[pl.ds((i // 8) * 64 + i % 8, 8, stride=8), :] = squares
 
             def between(i):
@@ -270,10 +270,15 @@
                     return get_high(p - 64, c)
                 return ux_ref[base + p]
 
-            def emit(i, squares):
+            def emit(i, squares, u, s):
                 gx_ref[pl.ds(w_row(0, i // 8, 8 * c) + i % 8, 8, stride=8), :] = squares
 
             column(load, lambda i: sx_ref[base + i], emit, 64)
+
+        def x_pair(n, t):
+            x_stream(t, 2 * n)
+            x_stream(t, 2 * n + 1)
+            return t
 
         def y_stream(t, q, parity, lows, highs, between):
             ib = 2 * q + parity
@@ -291,12 +296,10 @@
                     return jnp.where(lanes_low, roll(u_ref[aligned(base + h * 8), :]), halo)
                 return u_ref[aligned(base + p * 8), :]
 
-            def emit(j, squares):
+            def emit(j, squares, u, s):
                 rows = aligned(base + j * 8)
                 total = (squares + gx_ref[aligned(w_row(0, ib, j)), :]) + gz_ref[aligned(512 + base + j * 8), :]
                 size = total * lax.rsqrt(jnp.maximum(total, 1e-35))
-                s = s_ref[rows, :]
-                u = u_ref[rows, :]
                 moved = u + s * 3.0
                 moved = jnp.where(s > 0.0, moved - size, moved + size)
                 if stage == 1:
@@ -332,7 +335,7 @@
                 to_v([n_ref[aligned(w_row(t, ib, 16 * half + k)), :] for k in range(16)], t, ib, half)
 
         def tile(t, carry):
-            lax.fori_loop(0, 4, lambda c, kept: (x_stream(t, c), kept)[1], 0)
+            lax.fori_loop(0, 2, x_pair, t)
             lax.fori_loop(0, 4, lambda q, kept: (y_pair(t, q), kept)[1], 0)
             return carry
 
@@ -343,6 +346,21 @@
     section(0, wa, wb, x_faces0, y_faces0)
     section(1, wb, wc, x_faces1, y_faces1)
     section(2, wc, None, x_faces2, y_faces2)
+
+
+def finish(count_ref, moved_ref, out_ref, zero, sem):
+    def each(act, filled):
+        for t in range(SLOTS):
+            @pl.when((t < count_ref[0]) == filled)
+            def _():
+                source = moved_ref.at[t] if filled else zero
+                act(pltpu.make_async_copy(source, out_ref.at[t], sem.at[t]))
+
+    each(lambda copy: copy.start(), True)
+    zero[...] = jnp.zeros_like(zero)
+    each(lambda copy: copy.start(), False)
+    each(lambda copy: copy.wait(), True)
+    each(lambda copy: copy.wait(), False)
 
 
 def local(level_set, tile_count, neighbours):
@@ -370,8 +388,14 @@
         ),
         cost_estimate=pl.CostEstimate(flops=cells * 3 * 150, bytes_accessed=cells * 8, transcendentals=cells * 3),
     )(blocked, neighbours)
-    live = jnp.arange(SLOTS, dtype=jnp.int32) < tile_count[0]
-    return jnp.where(live[:, None, None], moved, 0.0)
+    return pl.pallas_call(
+        finish,
+        out_shape=jax.ShapeDtypeStruct(level_set.shape, jnp.float32),
+        in_specs=[pl.BlockSpec(memory_space=pltpu.SMEM), pl.BlockSpec(memory_space=pl.ANY)],
+        out_specs=pl.BlockSpec(memory_space=pl.ANY),
+        scratch_shapes=[pltpu.VMEM(level_set.shape[1:], jnp.float32), pltpu.SemaphoreType.DMA((SLOTS,))],
+        compiler_params=pltpu.CompilerParams(vmem_limit_bytes=8 * 2 ** 20),
+    )(tile_count, moved)
 
 
 def solution(mesh):

time: 86.4 us -> 85.5 us (0.990)
  other arithmetic: 2.49 us -> 0 us
  Pallas kernels: 82.5 us -> 84.1 us
    select_n x1 -> x0, other arithmetic: 2.49 us -> none  [local(): return jnp.where(live[:, None, None], moved, 0.0)]
    pallas_call x0 -> x1, Pallas kernels: none -> 2.04 us  [local(): pl.pallas_call(finish, out_shape=jax.ShapeDtypeStruct(level_set.shape, jn...]
where the time goes in v3:
time: 85.5 us; the launch traced here: 85.4 us
  Pallas kernels  84.1 us (98%)
    pallas_call x1, Pallas kernels, local(): pl.pallas_call(kernel, out_shape=jax.ShapeDtypeStruct(level_set.shape, jn...  82 us
    pallas_call x1, Pallas kernels, local(): pl.pallas_call(finish, out_shape=jax.ShapeDtypeStruct(level_set.shape, jn...  2.04 us

profile of v3, /device:TPU:1, one launch (start us, length us, event | category | flops | bytes accessed | tf_op | source)
XLA Modules:
  0.0 85.4 jit_solution(2849514606315230268)
XLA Ops:
  0.7 0.0 copy-start
  0.7 0.7 copy-done
  1.3 82.0 %shard_map.37.moved_ref = f32[4,64,4096]{2,1,0:T(8,128)S(1)} custom-call(f32[8192,128]{1,0:T(8,128)} %bitcast.5, s32[4,6]{1,0:T(4,128)S(1)} %copy-done), custom_call_target="tpu_custom_call" | custom-call | flops 471859200 | bytes 8388608 | tf_op jit(solution)/shard_map/pallas_call | solution.py:377
  83.4 2.0 %shard_map.38 = f32[4,64,4096]{2,1,0:T(8,128)} custom-call(s32[1]{0:T(128)S(6)} %copy.4.count_ref, f32[4,64,4096]{2,1,0:T(8,128)S(1)} %shard_map.37.moved_ref), custom_call_target="tpu_custom_call" | custom-call | tf_op jit(solution)/shard_map/pallas_call | solution.py:391
Async XLA Ops:
  0.7 0.7 copy-start

commit v4 on v3

--- a/solution.py
+++ b/solution.py
@@ -101,6 +101,7 @@
     v_rows = v_ref.reshape(SLOTS * 4 * EDGE * 8, 128)
     ux_rows = ux_ref.reshape(SLOTS * 4 * EDGE * 8, 128)
     sx_rows = sx_ref.reshape(SLOTS * 4 * EDGE * 8, 128)
+    sv_rows = sv_ref.reshape(SLOTS * 4 * EDGE * 8, 128)
 
     def x_rows(t, ib, j):
         return pl.ds(v_block(t, j // 8, ib * 8) * 8 + j % 8, 8, stride=8)
@@ -123,14 +124,17 @@
     for device in around:
         pl.semaphore_signal(barrier, inc=1, device_id=device, device_id_type=pl.DeviceIdType.MESH)
 
-    def to_v(values, t, ib, half):
+    def to_v(values, t, ib, half, with_sign=False):
         turned = jnp.concatenate(values, axis=0).T
         for jh in range(2):
             line = lax.rem(ib, 2) * 4 + half * 2 + jh
             for m in range(8):
                 r = jh * 64 + 8 * m
                 start = v_block(t, ib // 2, 8 * m) * 8 + line
-                v_rows[pl.ds(start, 8, stride=8), :] = turned[r:r + 8]
+                u = turned[r:r + 8]
+                v_rows[pl.ds(start, 8, stride=8), :] = u
+                if with_sign:
+                    sv_rows[pl.ds(start, 8, stride=8), :] = (u * scale_s) * lax.rsqrt(u * u + 1.0)
 
     def enter_block(t, ib):
         values = []
@@ -147,7 +151,7 @@
             ux_rows[x_rows(t, ib, j), :] = u
             sx_rows[x_rows(t, ib, j), :] = s
         for half in range(2):
-            to_v(values[16 * half:16 * half + 16], t, ib, half)
+            to_v(values[16 * half:16 * half + 16], t, ib, half, True)
 
     for t in range(SLOTS):
         def enter(q, carry, t=t):
@@ -158,13 +162,6 @@
         loads[t].wait()
         lax.fori_loop(0, 4, enter, 0)
 
-    def turned_sign(it, carry):
-        for k in range(64):
-            u = v_ref[it * 64 + k]
-            sv_ref[it * 64 + k] = (u * scale_s) * lax.rsqrt(u * u + 1.0)
-        return carry
-
-    lax.fori_loop(0, 16, turned_sign, 0)
     gvb[...] = jnp.zeros_like(gvb)
     pl.semaphore_wait(barrier, 4)
 

time: 85.5 us -> 85.4 us (level)
  no operation moved by 1% of the time
where the time goes in v4:
time: 85.4 us; the launch traced here: 85.2 us
  Pallas kernels  83.9 us (98%)
    pallas_call x1, Pallas kernels, local(): pl.pallas_call(kernel, out_shape=jax.ShapeDtypeStruct(level_set.shape, jn...  81.9 us
    pallas_call x1, Pallas kernels, local(): pl.pallas_call(finish, out_shape=jax.ShapeDtypeStruct(level_set.shape, jn...  2.04 us

profile of v4, /device:TPU:1, one launch (start us, length us, event | category | flops | bytes accessed | tf_op | source)
XLA Modules:
  0.0 85.2 jit_solution(9033210344577723067)
XLA Ops:
  0.7 0.0 copy-start
  0.7 0.7 copy-done
  1.3 81.9 %shard_map.37.moved_ref = f32[4,64,4096]{2,1,0:T(8,128)S(1)} custom-call(f32[8192,128]{1,0:T(8,128)} %bitcast.5, s32[4,6]{1,0:T(4,128)S(1)} %copy-done), custom_call_target="tpu_custom_call" | custom-call | flops 471859200 | bytes 8388608 | tf_op jit(solution)/shard_map/pallas_call | solution.py:374
  83.2 2.0 %shard_map.38 = f32[4,64,4096]{2,1,0:T(8,128)} custom-call(s32[1]{0:T(128)S(6)} %copy.4.count_ref, f32[4,64,4096]{2,1,0:T(8,128)S(1)} %shard_map.37.moved_ref), custom_call_target="tpu_custom_call" | custom-call | tf_op jit(solution)/shard_map/pallas_call | solution.py:388
Async XLA Ops:
  0.7 0.7 copy-start
